TPU v7x, 32 devices: a whole 2x2x4 slice. The times are simulated.
32 devices in a mesh: groups: 2 (over x), vid: 8 (over z, y), tok: 2 (over core).
Axes of the slice: x: 2, y: 2, z: 4, core: 2. Of those that a mesh axis runs over, the one named last changes fastest.
Arguments:
- captions: bfloat16 [16, 128, 32, 128], P(('groups', 'vid')), parts along dimension 0, may hold values from -8 to 8
- caption_lengths: int32 [16, 128], P(('groups', 'vid')), parts along dimension 0, may hold values from 1 to 32
- video_bank: bfloat16 [192, 256, 128], P(('groups', 'vid'), 'tok'), parts along dimension 0, may hold values from -1.5 to 1.5
- owner_order: int32 [6], P('groups'), parts along dimension 0, may hold values from 0 to 7, as said below
Outputs:
- scores: float32 [192, 384], P(('groups', 'vid')), parts along dimension 0
There are 2 independent parts, one for each index of `groups`. A program takes and returns all parts, laid end to end along the dimension named above; each array names one. Nothing has to cross between parts.
Inputs may be any that keep to these rules, and one draw needn't show every extreme that they name: `caption_lengths`: token slot j of a caption is real when j is less than its count. `owner_order`: 3 different block indices.
All inputs are finite; a program needn't handle non-finite values.
Results may differ from a plain program's by a relative error of at most 0.0003.
Values may be sent and summed in bfloat16 or wider, within the bound.
A program may use at most 64 MiB of HBM per device.

v0:
```python
import jax
import jax.numpy as jnp
from jax import lax
from jax.sharding import PartitionSpec as P

ROUNDS = 3


sharpness_factor = 5.0


def spread(value, axis, source):
    kept = jnp.where(lax.axis_index(axis) == source, value, 0).astype(value.dtype)
    return lax.psum(kept, axis)


def mask_weights(counts, slot_count):
    slots = jnp.arange(slot_count, dtype=jnp.int32)
    lengths_float = counts.astype(jnp.float32)
    return (slots[None, :] < counts[:, None]).astype(jnp.float32) / lengths_float[:, None]


def per_device(captions, caption_lengths, video_bank, owner_order):
    results = []
    bank_whole = lax.all_gather(video_bank, "tok", axis=1, tiled=True)
    share_rows = captions.shape[1] // lax.axis_size("tok")
    start_row = lax.axis_index("tok") * share_rows
    for round_index in range(ROUNDS):
        owner_now = owner_order[round_index]
        my_share = lax.dynamic_slice_in_dim(captions[0], start_row, share_rows, 0)
        my_counts = lax.dynamic_slice_in_dim(caption_lengths[0], start_row, share_rows, 0)
        share_rows_now, share_counts = (
            spread(my_share, "vid", owner_now),
            spread(my_counts, "vid", owner_now),
        )
        slot_count = share_rows_now.shape[1]
        query_rows = share_rows_now.reshape(share_rows * slot_count, share_rows_now.shape[2])

        def whole_video(footage_key_matrix):
            raw_similarity = (
                lax.dot_general(
                    query_rows,
                    footage_key_matrix,
                    (((1,), (1,)), ((), ())),
                    preferred_element_type=jnp.float32,
                )
                * sharpness_factor
            )
            row_peak = jnp.max(raw_similarity, axis=1)
            row_accumulated = jnp.sum(jnp.exp(raw_similarity - row_peak[:, None]), axis=1)
            return (row_peak + jnp.log(row_accumulated)) / sharpness_factor

        smoothed_scores = lax.map(whole_video, bank_whole).reshape(
            video_bank.shape[0], share_rows, slot_count
        )
        weights = mask_weights(share_counts, slot_count)
        results.append(
            jnp.einsum("vcj,cj->vc", smoothed_scores, weights, precision=lax.Precision.HIGHEST)
        )
    stacked = jnp.stack(results, axis=1)
    gathered = lax.all_gather(stacked, "tok", axis=2, tiled=True)
    return gathered.reshape(video_bank.shape[0], ROUNDS * captions.shape[1])


def solution(mesh):
    return jax.shard_map(
        per_device,
        mesh=mesh,
        in_specs=(
            P(("groups", "vid"), None, None, None),
            P(("groups", "vid"), None),
            P(("groups", "vid"), "tok", None),
            P("groups"),
        ),
        out_specs=P(("groups", "vid"), None),
        check_vma=False,
    )
```

profile of v0, /device:TPU:0, one launch (start us, length us, event | category | flops | bytes accessed | tf_op | source)
XLA Modules:
  0.0 167.4 jit_solution(8382262049726424937)
XLA Ops:
  6.5 1.4 fusion.21
  9.9 2.3 %broadcast_select_fusion.2 = (bf16[1,64,32,128]{3,2,1,0:T(8,128)(2,1)}, bf16[1,64,32,128]{3,2,1,0:T(8,128)(2,1)}, bf16[1,64,32,128]{3,2,1,0:T(8,128)(2,1)}) fusion(pred[]{:T(512)S(6)} %eq.12, bf16[1,128,32,128]{3,2,1,0:T(8,128)(2,1)} %param.10, s32[]{:T(128)S(6)} %select_n.67, pred[]{:T(512)S(6)} %eq.13, pred[]{:T(512)S(6)} %eq.14), kind=kLoop, calls=%fused_computation.26 | loop fusion | flops 786432 | bytes 2097159 | tf_op jit(solution)/shard_map/jit(_where)/select_n | solution.py:13
  12.3 13.2 %all-reduce = (s32[64]{0:T(128)S(1)}, s32[64]{0:T(128)S(1)}, s32[64]{0:T(128)S(1)}) all-reduce(s32[64]{0:T(128)S(1)} %get-tuple-element.115, s32[64]{0:T(128)S(1)} %get-tuple-element.114, s32[64]{0:T(128)S(1)} %get-tuple-element.113), channel_id=1, replica_groups=mesh['groups'=2,'vid'=8,'tok'=2] {'vid'}, use_global_device_ids=true, to_apply=%region_12.13 | all-reduce | flops 192 | bytes 1536 | tf_op jit(solution)/shard_map/psum | solution.py:14
  25.5 2.4 %all_gather.6 = bf16[12,256,128]{2,1,0:T(8,128)(2,1)S(1)} all-gather(bf16[12,128,128]{2,1,0:T(8,128)(2,1)S(1)} %copy-done.2), channel_id=1, replica_groups=mesh['groups'=2,'vid'=8,'tok'=2] {'tok'}, dimensions={1}, use_global_device_ids=true | all-gather | bytes 1179648 | tf_op jit(solution)/shard_map/all_gather | solution.py:25
  28.1 76.8 %all-reduce.4.cloned.1.call-done = (bf16[2048,128]{1,0:T(8,128)(2,1)}, bf16[2048,128]{1,0:T(8,128)(2,1)}, bf16[2048,128]{1,0:T(8,128)(2,1)}) async-done(((bf16[2048,128]{1,0:T(8,128)(2,1)}, bf16[2048,128]{1,0:T(8,128)(2,1)}, bf16[2048,128]{1,0:T(8,128)(2,1)}), (bf16[2048,128]{1,0:T(8,128)(2,1)}, bf16[2048,128]{1,0:T(8,128)(2,1)}, bf16[2048,128]{1,0:T(8,128)(2,1)})) %all-reduce.4.cloned.1.call-update) | async-done | bytes 1572880 | tf_op jit(solution)/shard_map/psum | solution.py:14
  104.9 24.6 %while.30 = (s32[]{:T(128)}, f32[12,2048]{1,0:T(8,128)S(1)}, bf16[12,256,128]{2,1,0:T(8,128)(2,1)S(1)}, bf16[2048,128]{1,0:T(8,128)(2,1)}, s32[]{:T(128)}, /*index=5*/s32[]{:T(128)}) while((s32[]{:T(128)}, f32[12,2048]{1,0:T(8,128)S(1)}, bf16[12,256,128]{2,1,0:T(8,128)(2,1)S(1)}, bf16[2048,128]{1,0:T(8,128)(2,1)}, s32[]{:T(128)}, ...), condition=%wide.region_5.6_spmd, body=%wide.region_2.5_spmd.sunk | while | flops 136314880 | bytes 4849741 | solution.py:53
  104.9 1.5 fusion.35
  107.0 1.5 fusion.35
  109.1 1.5 fusion.35
  111.1 1.5 fusion.35
  113.2 1.5 fusion.35
  115.2 1.5 fusion.35
  117.3 1.5 fusion.35
  119.3 1.5 fusion.35
  121.3 1.5 fusion.35
  123.4 1.5 fusion.35
  125.4 1.5 fusion.35
  127.5 1.5 fusion.35
  129.7 1.1 fusion.13
  130.9 12.0 %while.31 = (s32[]{:T(128)}, f32[12,2048]{1,0:T(8,128)S(1)}, bf16[12,256,128]{2,1,0:T(8,128)(2,1)S(1)}, bf16[2048,128]{1,0:T(8,128)(2,1)S(1)}, s32[]{:T(128)}, /*index=5*/s32[]{:T(128)}) while((s32[]{:T(128)}, f32[12,2048]{1,0:T(8,128)S(1)}, bf16[12,256,128]{2,1,0:T(8,128)(2,1)S(1)}, bf16[2048,128]{1,0:T(8,128)(2,1)S(1)}, s32[]{:T(128)}, ...), condition=%wide.region_11.12_spmd, body=%wide.region_8.11_spmd.sunk | while | flops 136314880 | bytes 4849741 | solution.py:53
  130.9 0.4 fusion.37
  131.9 0.4 fusion.37
  143.1 1.1 fusion.11
  144.3 12.0 %while.32 = (s32[]{:T(128)}, f32[12,2048]{1,0:T(8,128)S(1)}, bf16[12,256,128]{2,1,0:T(8,128)(2,1)S(1)}, bf16[2048,128]{1,0:T(8,128)(2,1)S(1)}, s32[]{:T(128)}, /*index=5*/s32[]{:T(128)}) while((s32[]{:T(128)}, f32[12,2048]{1,0:T(8,128)S(1)}, bf16[12,256,128]{2,1,0:T(8,128)(2,1)S(1)}, bf16[2048,128]{1,0:T(8,128)(2,1)S(1)}, s32[]{:T(128)}, ...), condition=%wide.region_17.18_spmd, body=%wide.region_14.17_spmd.sunk | while | flops 136314880 | bytes 4849741 | solution.py:53
  144.3 0.4 fusion.39
  145.3 0.4 fusion.39
  146.3 0.4 fusion.39
  147.3 0.4 fusion.39
  148.3 0.4 fusion.39
  156.5 1.1 fusion.9
  157.8 2.0 %all_gather.7 = f32[12,3,128]{0,1,2:T(4,128)S(1)} all-gather(f32[12,3,64]{0,1,2:T(4,128)S(1)} %copy.6), channel_id=1, replica_groups=mesh['groups'=2,'vid'=8,'tok'=2] {'tok'}, dimensions={2}, use_global_device_ids=true | all-gather | bytes 27648 | tf_op jit(solution)/shard_map/all_gather | solution.py:61
  160.0 0.6 copy.17
  (154 shorter events, 27.7 us)
Async XLA Ops:
  6.5 5.7 %copy-start.3 = (s32[1,128]{1,0:T(1,128)S(1)}, s32[1,128]{1,0:T(1,128)}, u32[]{:S(2)}) copy-start(s32[1,128]{1,0:T(1,128)} %param.11) | copy-start | bytes 1540
  6.5 19.0 %copy-start.2 = (bf16[12,128,128]{2,1,0:T(8,128)(2,1)S(1)}, bf16[12,128,128]{2,1,0:T(8,128)(2,1)}, u32[]{:S(2)}) copy-start(bf16[12,128,128]{2,1,0:T(8,128)(2,1)} %param.12) | copy-start | bytes 1179652
  6.5 98.4 %all-reduce.4.cloned.1.call-start = ((), (), s32[]{:S(2)}) async-start(), calls=%async_computation | async-start | bytes 3145728 | tf_op jit(solution)/shard_map/psum | solution.py:14
  104.9 26.0 %copy-start.1 = (bf16[2048,128]{1,0:T(8,128)(2,1)S(1)}, bf16[2048,128]{1,0:T(8,128)(2,1)}, u32[]{:S(2)}) copy-start(bf16[2048,128]{1,0:T(8,128)(2,1)} %get-tuple-element.229) | copy-start | bytes 1572868
  130.9 13.4 %copy-start = (bf16[2048,128]{1,0:T(8,128)(2,1)S(1)}, bf16[2048,128]{1,0:T(8,128)(2,1)}, u32[]{:S(2)}) copy-start(bf16[2048,128]{1,0:T(8,128)(2,1)} %get-tuple-element.211) | copy-start | bytes 1572868
Sparse Core Ops, SparseCore 0:
  12.3 92.5 all-reduce.3
where the time goes:
time: 168 us; the launch traced here: 167 us
  waiting for transfers between devices  76.8 us (46%)
  matrix products  31.9 us (19%)
  blocking collectives  17.6 us (10%)
  between operations  15.4 us (9%)
  other arithmetic  14.1 us (8%)
  local copies, waits for them, and re-layouts  10.4 us (6%)
    psum x1, waiting for transfers between devices, spread(): return lax.psum(kept, axis)  76.8 us
    dot_general x36, matrix products, whole_video(): lax.dot_general(query_rows, footage_key_matrix, (((1,), (1,)), ((), ())),...  28.5 us
    psum x1, blocking collectives, spread(): return lax.psum(kept, axis)  13.2 us
    reduce_sum x36, other arithmetic, whole_video(): jnp.sum(jnp.exp(raw_similarity - row_peak[:, None]), axis=1)  11.1 us
    dynamic_update_slice x36, local copies, waits for them, and re-layouts, per_device(): lax.map(whole_video, bank_whole)  7.37 us
  transfers between devices with their start and end apart: 1, of which 1 were waited for; matrix products, arithmetic and copies ran while one was open for 0% of the time, Pallas kernels for 0%

commit v1 on v0

v1 whole, which is shorter than its diff:
```python
import functools
import math

import jax
import jax.numpy as jnp
from jax import lax
from jax.experimental import pallas as pl
from jax.experimental.pallas import tpu as pltpu
from jax.sharding import PartitionSpec as P

sharpness_factor = 5.0
SCALE = sharpness_factor * math.log2(math.e)
UNSCALE = math.log(2.0) / sharpness_factor

CHUNK_ROWS = 256
SKEW = 2
BANK_LAG = 4
MESH = pl.DeviceIdType.MESH


def kernel(
    n, rounds, slots,
    caps_ref, counts_ref, bank_ref, owner_ref, out_ref,
    mine, in_left, in_right, out_left, out_right, query, bank, counts_all, soft, acc, acc_in,
    own_sem, bank_sem, pair_send, pair_recv, right_send, right_recv, left_send, left_recv,
    count_send, count_recv, bank_send, bank_recv, acc_send, acc_recv,
):
    me = lax.axis_index("vid")
    tok = lax.axis_index("tok")
    place = me // 2
    side = me % 2
    mate = me + 1 - 2 * side
    other = 1 - tok
    line = n // 2
    subs = mine.shape[1]
    rows = mine.shape[2]
    chunks = subs * rounds
    videos = bank.shape[1]
    half = videos // 2
    mate_id = {"vid": mate, "tok": tok}
    twin_id = {"vid": me, "tok": other}
    cross_id = {"vid": mate, "tok": other}
    right_id = {"vid": me + 2, "tok": tok}
    left_id = {"vid": me - 2, "tok": tok}

    def remote(src, dst, send, recv, device):
        return pltpu.make_async_remote_copy(
            src_ref=src, dst_ref=dst, send_sem=send, recv_sem=recv,
            device_id=device, device_id_type=MESH,
        )

    def block_rows(of_side, sub):
        quarter = of_side * 2 + tok
        return pl.ds(pl.multiple_of((quarter * subs + sub) * rows, rows), rows)

    def own_copy(sub):
        return pltpu.make_async_copy(
            caps_ref.at[block_rows(side, sub)], mine.at[side, sub], own_sem.at[sub]
        )

    def pair_copy(sub):
        return remote(
            caps_ref.at[block_rows(1 - side, sub)], mine.at[side, sub],
            pair_send.at[sub], pair_recv.at[sub], mate_id,
        )

    def pair_arrival(sub):
        return remote(
            mine.at[1 - side, sub], mine.at[1 - side, sub],
            pair_send.at[sub], pair_recv.at[sub], mate_id,
        )

    def part(i):
        return pl.ds(i * half, half)

    bank_own = pltpu.make_async_copy(bank_ref, bank.at[0, :, tok], bank_sem)
    bank_twin = remote(
        bank_ref, bank.at[0, :, tok], bank_send.at[0], bank_recv.at[0], twin_id
    )

    def bank_pair(i):
        return remote(
            bank_ref.at[part(i)], bank.at[1, part(i), tok],
            bank_send.at[1 + i], bank_recv.at[1 + i], mate_id,
        )

    def bank_relay(i):
        return remote(
            bank.at[1, part(i), tok], bank.at[1, part(i), tok],
            bank_send.at[3 + i], bank_recv.at[3 + i], twin_id,
        )

    def bank_relayed(i):
        return remote(
            bank.at[1, part(i), other], bank.at[1, part(i), other],
            bank_send.at[3 + i], bank_recv.at[3 + i], twin_id,
        )

    def right_copy(k):
        return remote(
            out_right.at[k], in_left.at[k], right_send.at[k], right_recv.at[k], right_id
        )

    def left_copy(k):
        return remote(
            out_left.at[k], in_right.at[k], left_send.at[k], left_recv.at[k], left_id
        )

    def count_copy(to):
        return remote(
            counts_all.at[me], counts_all.at[me], count_send.at[to], count_recv.at[me],
            {"vid": to, "tok": tok},
        )

    def count_arrival(source):
        return remote(
            counts_all.at[source], counts_all.at[source], count_send.at[source],
            count_recv.at[source], {"vid": source, "tok": tok},
        )

    barrier = pltpu.get_barrier_semaphore()

    def greet(j, _):
        to = lax.rem(me + j, n)
        pl.semaphore_signal(barrier, inc=1, device_id={"vid": to, "tok": tok}, device_id_type=MESH)
        return 0

    lax.fori_loop(1, n, greet, 0)
    for device in (twin_id, cross_id):
        pl.semaphore_signal(barrier, inc=1, device_id=device, device_id_type=MESH)
    for sub in range(subs):
        own_copy(sub).start()
    bank_own.start()
    counts_all[me] = counts_ref[...]
    acc[...] = jnp.zeros_like(acc)
    pl.semaphore_wait(barrier, n + 1)

    pair_copy(0).start()

    def push(j, _):
        count_copy(lax.rem(me + j, n)).start()
        return 0

    lax.fori_loop(1, n, push, 0)
    bank_twin.start()

    def owner_of(k):
        return owner_ref[lax.rem(k, rounds)]

    def candidate(k):
        sub = k // rounds
        owner_side = jnp.full((rows, mine.shape[3]), lax.rem(owner_of(k), 2), jnp.int32)
        return jnp.where(
            owner_side == 0,
            mine[0, sub].astype(jnp.float32),
            mine[1, sub].astype(jnp.float32),
        )

    def owner_place(k):
        return jnp.full((rows, mine.shape[3]), owner_of(k) // 2, jnp.int32)

    def pick(k, incoming):
        return jnp.where(
            owner_place(k) == place, candidate(k), incoming.astype(jnp.float32)
        ).astype(jnp.bfloat16)

    def score(k, slot):
        q = query[k]
        group = 2

        def body(step, _):
            base = step * group
            tokens = bank[slot, pl.ds(base, group)]
            tokens = tokens.reshape(group * tokens.shape[1] * tokens.shape[2], tokens.shape[3])
            s = lax.dot_general(
                tokens, q, (((1,), (1,)), ((), ())), preferred_element_type=jnp.float32
            )
            s = s.reshape(group, s.shape[0] // group, rows)
            for g in range(group):
                sv = s[g]
                peak = jnp.max(sv, axis=0, keepdims=True)
                total = jnp.sum(jnp.exp2((sv - peak) * SCALE), axis=0, keepdims=True)
                soft[pl.ds(base + g, 1), :] = peak + UNSCALE * jnp.log2(total)
            return 0

        lax.fori_loop(0, videos // group, body, 0, unroll=2)
        r = lax.rem(k, rounds)
        first = ((side * 2 + tok) * subs + k // rounds) * (rows // slots)
        width = acc.shape[3]
        row = lax.broadcasted_iota(jnp.int32, (rows, width), 0)
        column = lax.broadcasted_iota(jnp.int32, (rows, width), 1)
        counts = counts_all[owner_of(k)]
        keep = (column == first + row // slots) & (row % slots < counts)
        keep = jnp.where(keep, 1.0, 0.0).astype(jnp.bfloat16)
        values = soft[...]
        high = values.astype(jnp.bfloat16)
        low = (values - high.astype(jnp.float32)).astype(jnp.bfloat16)
        acc[slot, r] += jnp.dot(high, keep, preferred_element_type=jnp.float32) + jnp.dot(
            low, keep, preferred_element_type=jnp.float32
        )

    near = jnp.minimum(place, line - 1 - place)
    far = jnp.maximum(place, line - 1 - place)

    def step_body(step, _):
        first_use = step - SKEW * near
        sub_now = first_use // rounds

        @pl.when((first_use >= 0) & (first_use < chunks) & (lax.rem(first_use + rounds, rounds) == 0))
        def _():
            own_copy(sub_now).wait()
            pair_arrival(sub_now).wait_recv()

            @pl.when(sub_now + 1 < subs)
            def _():
                pair_copy(sub_now + 1).start()

            for i in range(2):
                @pl.when(sub_now == i)
                def _():
                    bank_pair(i).start()

        k_right = step - SKEW * place

        @pl.when((k_right >= 0) & (k_right < chunks))
        def _():
            @pl.when(place > 0)
            def _():
                right_copy(k_right).wait_recv()

            @pl.when(place < line - 1)
            def _():
                out_right[k_right] = pick(k_right, in_left[k_right])
                right_copy(k_right).start()

        k_left = step - SKEW * (line - 1 - place)

        @pl.when((k_left >= 0) & (k_left < chunks))
        def _():
            @pl.when(place < line - 1)
            def _():
                left_copy(k_left).wait_recv()

            @pl.when(place > 0)
            def _():
                out_left[k_left] = pick(k_left, in_right[k_left])
                left_copy(k_left).start()

        k = step - SKEW * far

        @pl.when(k == 0)
        def _():
            bank_own.wait()
            bank_twin.wait_recv()

            def arrive(j, _):
                count_arrival(lax.rem(me + j, n)).wait_recv()
                return 0

            lax.fori_loop(1, n, arrive, 0)

        for i in range(2):
            @pl.when(k == BANK_LAG - 2 + i)
            def _():
                bank_pair(i).wait_recv()
                bank_relay(i).start()

        @pl.when(k == BANK_LAG)
        def _():
            for i in range(2):
                bank_relayed(i).wait_recv()

        @pl.when((k >= 0) & (k < chunks))
        def _():
            travelled = jnp.where(
                owner_place(k) < place,
                in_left[k].astype(jnp.float32),
                in_right[k].astype(jnp.float32),
            )
            query[k] = pick(k, travelled)
            score(k, 0)

        k_late = k - BANK_LAG

        @pl.when((k_late >= 0) & (k_late < chunks))
        def _():
            score(k_late, 1)

        return 0

    lax.fori_loop(0, chunks + SKEW * (line - 1) + BANK_LAG, step_body, 0)

    sends = [
        remote(acc.at[0], acc_in.at[0], acc_send.at[0], acc_recv.at[0], twin_id),
        remote(acc.at[1], acc_in.at[1], acc_send.at[1], acc_recv.at[1], mate_id),
        remote(acc.at[1], acc_in.at[2], acc_send.at[2], acc_recv.at[2], cross_id),
    ]
    for send in sends:
        send.start()

    def sent(j, _):
        count_copy(lax.rem(me + j, n)).wait_send()
        return 0

    lax.fori_loop(1, n, sent, 0)
    for sub in range(subs):
        pair_copy(sub).wait_send()
    bank_twin.wait_send()
    for i in range(2):
        bank_pair(i).wait_send()
        bank_relay(i).wait_send()

    def drain(k, _):
        @pl.when(place < line - 1)
        def _():
            right_copy(k).wait_send()

        @pl.when(place > 0)
        def _():
            left_copy(k).wait_send()

        return 0

    lax.fori_loop(0, chunks, drain, 0)
    for send in sends:
        send.wait()
    width = acc.shape[3]
    for r in range(rounds):
        total = acc[0, r] + acc_in[0, r] + acc_in[1, r] + acc_in[2, r]
        counts = counts_all[owner_ref[r]].astype(jnp.float32)
        out_ref[:, r * width : (r + 1) * width] = total / counts


def per_device(captions, caption_lengths, video_bank, owner_order):
    n = lax.axis_size("vid")
    parts = 2 * lax.axis_size("tok")
    _, blocks, slots, depth = captions.shape
    videos, tokens, _ = video_bank.shape
    rounds = owner_order.shape[0]
    rows = CHUNK_ROWS
    subs = blocks * slots // parts // rows
    chunks = subs * rounds
    bf16, f32 = jnp.bfloat16, jnp.float32
    stream = pltpu.VMEM((chunks, rows, depth), bf16)
    dma = pltpu.SemaphoreType.DMA
    logits = rounds * (blocks * slots // parts) * 2 * videos * 2 * tokens
    return pl.pallas_call(
        functools.partial(kernel, n, rounds, slots),
        out_shape=jax.ShapeDtypeStruct((videos, rounds * blocks), f32),
        in_specs=[
            pl.BlockSpec(memory_space=pl.ANY),
            pl.BlockSpec(memory_space=pltpu.VMEM),
            pl.BlockSpec(memory_space=pl.ANY),
            pl.BlockSpec(memory_space=pltpu.SMEM),
        ],
        out_specs=pl.BlockSpec(memory_space=pltpu.VMEM),
        scratch_shapes=[
            pltpu.VMEM((2, subs, rows, depth), bf16),
            stream, stream, stream, stream, stream,
            pltpu.VMEM((2, videos, 2, tokens, depth), bf16),
            pltpu.VMEM((n, 1, blocks), jnp.int32),
            pltpu.VMEM((videos, rows), f32),
            pltpu.VMEM((2, rounds, videos, blocks), f32),
            pltpu.VMEM((3, rounds, videos, blocks), f32),
            dma((subs,)), dma, dma((subs,)), dma((subs,)),
            dma((chunks,)), dma((chunks,)), dma((chunks,)), dma((chunks,)),
            dma((n,)), dma((n,)), dma((5,)), dma((5,)), dma((3,)), dma((3,)),
        ],
        compiler_params=pltpu.CompilerParams(
            collective_id=0, has_side_effects=True, vmem_limit_bytes=40 * 1024 * 1024
        ),
        cost_estimate=pl.CostEstimate(
            flops=2 * depth * logits, bytes_accessed=8 * 1024 * 1024, transcendentals=logits
        ),
    )(captions.reshape(blocks * slots, depth), caption_lengths, video_bank, owner_order)


def solution(mesh):
    return jax.shard_map(
        per_device,
        mesh=mesh,
        in_specs=(
            P(("groups", "vid"), None, None, None),
            P(("groups", "vid"), None),
            P(("groups", "vid"), "tok", None),
            P("groups"),
        ),
        out_specs=P(("groups", "vid"), None),
        check_vma=False,
    )
```

time: 168 us -> 66.4 us (0.40)
  waiting for transfers between devices: 76.8 us -> 0 us
  Pallas kernels: 0 us -> 62.7 us
  matrix products: 31.9 us -> 0 us
  blocking collectives: 17.6 us -> 0 us
  between operations: 15.4 us -> 0.01 us
  other arithmetic: 14.1 us -> 0 us
  local copies, waits for them, and re-layouts: 10.4 us -> 3.5 us
    psum x1 -> x0, waiting for transfers between devices: 76.8 us -> none  [spread(): return lax.psum(kept, axis)]
    pallas_call x0 -> x1, Pallas kernels: none -> 62.7 us  [per_device(): pl.pallas_call(functools.partial(kernel, n, rounds, slots), out_shape=jax...]
    dot_general x39 -> x0, matrix products: 31.9 us -> none  [the longest x36 28.5 us: whole_video(): lax.dot_general(query_rows, footage_key_matrix, (((1,), (1,)), ((), ())),...]
    psum x1 -> x0, blocking collectives: 13.2 us -> none  [spread(): return lax.psum(kept, axis)]
    reduce_sum x36 -> x0, other arithmetic: 11.1 us -> none  [whole_video(): jnp.sum(jnp.exp(raw_similarity - row_peak[:, None]), axis=1)]
    dynamic_update_slice x36 -> x0, local copies, waits for them, and re-layouts: 7.37 us -> none  [per_device(): lax.map(whole_video, bank_whole)]
    all_gather x2 -> x0, blocking collectives: 4.36 us -> none  [the longest x1 2.37 us: per_device(): bank_whole = lax.all_gather(video_bank, 'tok', axis=1, tiled=True)]
    unnamed x10 -> x9, local copies, waits for them, and re-layouts: 0.66 us -> 3.5 us
  transfers between devices with their start and end apart: 1 -> 0, of which waited for: 1 -> 0; matrix products, arithmetic and copies ran while one was open for 0% -> 0% of each run, Pallas kernels for 0% -> 0%
where the time goes in v1:
time: 66.4 us; the launch traced here: 66.2 us
  Pallas kernels  62.7 us (94%)
  local copies, waits for them, and re-layouts  3.5 us (5%)
    pallas_call x1, Pallas kernels, per_device(): pl.pallas_call(functools.partial(kernel, n, rounds, slots), out_shape=jax...  62.7 us
    unnamed x9, local copies, waits for them, and re-layouts  3.5 us

profile of v1, /device:TPU:0, one launch (start us, length us, event | category | flops | bytes accessed | tf_op | source)
XLA Modules:
  0.0 66.2 jit_solution(2587477679099484810)
XLA Ops:
  0.0 0.0 copy-start.3
  0.0 0.0 copy-start.2
  0.0 0.7 copy-done.3
  0.7 0.0 copy-done.2
  0.7 0.0 copy-start
  0.7 1.2 %copy-done = bf16[1,128,32,128]{3,2,1,0:T(8,128)(2,1)S(1)} copy-done((bf16[1,128,32,128]{3,2,1,0:T(8,128)(2,1)S(1)}, bf16[1,128,32,128]{3,2,1,0:T(8,128)(2,1)}, u32[]{:S(2)}) %copy-start) | copy-done | bytes 1048600
  1.9 0.0 copy-start.1
  1.9 1.0 %copy-done.1 = bf16[12,128,128]{2,1,0:T(8,128)(2,1)S(1)} copy-done((bf16[12,128,128]{2,1,0:T(8,128)(2,1)S(1)}, bf16[12,128,128]{2,1,0:T(8,128)(2,1)}, u32[]{:S(2)}) %copy-start.1) | copy-done | bytes 393240
  2.9 62.7 %shard_map.46 = f32[12,384]{1,0:T(8,128)S(1)} custom-call(bf16[4096,128]{1,0:T(8,128)(2,1)S(1)} %bitcast.1, s32[1,128]{1,0:T(1,128)S(1)} %copy-done.2, bf16[12,128,128]{2,1,0:T(8,128)(2,1)S(1)} %copy-done.1, s32[3]{0:T(128)S(1)} %copy-done.3), custom_call_target="tpu_custom_call" | custom-call | flops 4831838208 | bytes 8388608 | tf_op jit(solution)/shard_map/pallas_call | solution.py:347
  65.6 0.6 copy.6
Async XLA Ops:
  0.0 0.7 copy-start.3
  0.0 0.7 %copy-start.2 = (s32[1,128]{1,0:T(1,128)S(1)}, s32[1,128]{1,0:T(1,128)}, u32[]{:S(2)}) copy-start(s32[1,128]{1,0:T(1,128)} %counts_ref.1) | copy-start | bytes 1540
  0.7 1.2 %copy-start = (bf16[1,128,32,128]{3,2,1,0:T(8,128)(2,1)S(1)}, bf16[1,128,32,128]{3,2,1,0:T(8,128)(2,1)}, u32[]{:S(2)}) copy-start(bf16[1,128,32,128]{3,2,1,0:T(8,128)(2,1)} %param.4) | copy-start | bytes 3145732
  1.9 1.0 %copy-start.1 = (bf16[12,128,128]{2,1,0:T(8,128)(2,1)S(1)}, bf16[12,128,128]{2,1,0:T(8,128)(2,1)}, u32[]{:S(2)}) copy-start(bf16[12,128,128]{2,1,0:T(8,128)(2,1)} %bank_ref.1) | copy-start | bytes 1179652

commit v2 on v1

--- a/solution.py
+++ b/solution.py
@@ -165,25 +165,20 @@
         ).astype(jnp.bfloat16)
 
     def score(k, slot):
-        q = query[k]
-        group = 2
-
-        def body(step, _):
-            base = step * group
-            tokens = bank[slot, pl.ds(base, group)]
-            tokens = tokens.reshape(group * tokens.shape[1] * tokens.shape[2], tokens.shape[3])
-            s = lax.dot_general(
-                tokens, q, (((1,), (1,)), ((), ())), preferred_element_type=jnp.float32
-            )
-            s = s.reshape(group, s.shape[0] // group, rows)
-            for g in range(group):
-                sv = s[g]
-                peak = jnp.max(sv, axis=0, keepdims=True)
-                total = jnp.sum(jnp.exp2((sv - peak) * SCALE), axis=0, keepdims=True)
-                soft[pl.ds(base + g, 1), :] = peak + UNSCALE * jnp.log2(total)
-            return 0
-
-        lax.fori_loop(0, videos // group, body, 0, unroll=2)
+        q = query[k].T
+
+        def similarity(v):
+            tokens = bank[slot, v].reshape(bank.shape[2] * bank.shape[3], bank.shape[4])
+            return jnp.dot(tokens, q, preferred_element_type=jnp.float32)
+
+        ahead = similarity(0)
+        for v in range(videos):
+            now = ahead
+            if v + 1 < videos:
+                ahead = similarity(v + 1)
+            peak = jnp.max(now, axis=0, keepdims=True)
+            total = jnp.sum(jnp.exp2((now - peak) * SCALE), axis=0, keepdims=True)
+            soft[v : v + 1, :] = peak + UNSCALE * jnp.log2(total)
         r = lax.rem(k, rounds)
         first = ((side * 2 + tok) * subs + k // rounds) * (rows // slots)
         width = acc.shape[3]
@@ -348,9 +343,9 @@
         functools.partial(kernel, n, rounds, slots),
         out_shape=jax.ShapeDtypeStruct((videos, rounds * blocks), f32),
         in_specs=[
-            pl.BlockSpec(memory_space=pl.ANY),
+            pl.BlockSpec(memory_space=pltpu.HBM),
             pl.BlockSpec(memory_space=pltpu.VMEM),
-            pl.BlockSpec(memory_space=pl.ANY),
+            pl.BlockSpec(memory_space=pltpu.HBM),
             pl.BlockSpec(memory_space=pltpu.SMEM),
         ],
         out_specs=pl.BlockSpec(memory_space=pltpu.VMEM),

time: 66.4 us -> 57.6 us (0.87)
  Pallas kernels: 62.7 us -> 53.9 us
    pallas_call x1, Pallas kernels: 62.7 us -> 53.9 us  [per_device(): pl.pallas_call(functools.partial(kernel, n, rounds, slots), out_shape=jax...]
where the time goes in v2:
time: 57.6 us; the launch traced here: 57.4 us
  Pallas kernels  53.9 us (94%)
  local copies, waits for them, and re-layouts  3.5 us (6%)
    pallas_call x1, Pallas kernels, per_device(): pl.pallas_call(functools.partial(kernel, n, rounds, slots), out_shape=jax...  53.9 us
    unnamed x9, local copies, waits for them, and re-layouts  3.5 us

profile of v2, /device:TPU:0, one launch (start us, length us, event | category | flops | bytes accessed | tf_op | source)
XLA Modules:
  0.0 57.4 jit_solution(14785462360077500297)
XLA Ops:
  0.0 0.0 copy-start.3
  0.0 0.0 copy-start.2
  0.0 0.7 %copy-done.3 = s32[3]{0:T(128)S(1)} copy-done((s32[3]{0:T(128)S(1)}, s32[3]{0:T(128)}, u32[]{:S(2)}) %copy-start.3) | copy-done | bytes 36
  0.7 0.0 copy-done.2
  0.7 0.0 copy-start
  0.7 1.2 %copy-done = bf16[1,128,32,128]{3,2,1,0:T(8,128)(2,1)S(1)} copy-done((bf16[1,128,32,128]{3,2,1,0:T(8,128)(2,1)S(1)}, bf16[1,128,32,128]{3,2,1,0:T(8,128)(2,1)}, u32[]{:S(2)}) %copy-start) | copy-done | bytes 1048600
  1.9 0.0 copy-start.1
  1.9 1.0 %copy-done.1 = bf16[12,128,128]{2,1,0:T(8,128)(2,1)S(1)} copy-done((bf16[12,128,128]{2,1,0:T(8,128)(2,1)S(1)}, bf16[12,128,128]{2,1,0:T(8,128)(2,1)}, u32[]{:S(2)}) %copy-start.1) | copy-done | bytes 393240
  2.9 53.9 %shard_map.46 = f32[12,384]{1,0:T(8,128)S(1)} custom-call(bf16[4096,128]{1,0:T(8,128)(2,1)S(1)} %bitcast.1, s32[1,128]{1,0:T(1,128)S(1)} %copy-done.2, bf16[12,128,128]{2,1,0:T(8,128)(2,1)S(1)} %copy-done.1, s32[3]{0:T(128)S(1)} %copy-done.3), custom_call_target="tpu_custom_call" | custom-call | flops 4831838208 | bytes 8388608 | tf_op jit(solution)/shard_map/pallas_call | solution.py:342
  56.8 0.6 %copy.6 = f32[12,384]{1,0:T(8,128)} copy(f32[12,384]{1,0:T(8,128)S(1)} %shard_map.46) | data formatting | bytes 36864
Async XLA Ops:
  0.0 0.7 %copy-start.3 = (s32[3]{0:T(128)S(1)}, s32[3]{0:T(128)}, u32[]{:S(2)}) copy-start(s32[3]{0:T(128)} %owner_ref.1) | copy-start | bytes 40
  0.0 0.7 %copy-start.2 = (s32[1,128]{1,0:T(1,128)S(1)}, s32[1,128]{1,0:T(1,128)}, u32[]{:S(2)}) copy-start(s32[1,128]{1,0:T(1,128)} %counts_ref.1) | copy-start | bytes 1540
  0.7 1.2 %copy-start = (bf16[1,128,32,128]{3,2,1,0:T(8,128)(2,1)S(1)}, bf16[1,128,32,128]{3,2,1,0:T(8,128)(2,1)}, u32[]{:S(2)}) copy-start(bf16[1,128,32,128]{3,2,1,0:T(8,128)(2,1)} %param.4) | copy-start | bytes 3145732
  1.9 1.0 %copy-start.1 = (bf16[12,128,128]{2,1,0:T(8,128)(2,1)S(1)}, bf16[12,128,128]{2,1,0:T(8,128)(2,1)}, u32[]{:S(2)}) copy-start(bf16[12,128,128]{2,1,0:T(8,128)(2,1)} %bank_ref.1) | copy-start | bytes 1179652

commit v3 on v2

--- a/solution.py
+++ b/solution.py
@@ -21,7 +21,7 @@
 def kernel(
     n, rounds, slots,
     caps_ref, counts_ref, bank_ref, owner_ref, out_ref,
-    mine, in_left, in_right, out_left, out_right, query, bank, counts_all, soft, acc, acc_in,
+    mine, in_left, in_right, out_left, out_right, query, bank, counts_all, peaks, sums, soft, acc, acc_in,
     own_sem, bank_sem, pair_send, pair_recv, right_send, right_recv, left_send, left_recv,
     count_send, count_recv, bank_send, bank_recv, acc_send, acc_recv,
 ):
@@ -166,18 +166,26 @@
 
     def score(k, slot):
         q = query[k].T
-
-        def similarity(v):
-            tokens = bank[slot, v].reshape(bank.shape[2] * bank.shape[3], bank.shape[4])
-            return jnp.dot(tokens, q, preferred_element_type=jnp.float32)
+        tiles = bank.shape[2]
+
+        def similarity(b):
+            return jnp.dot(
+                bank[slot, b // tiles, b % tiles], q, preferred_element_type=jnp.float32
+            )
 
         ahead = similarity(0)
+        for b in range(videos * tiles):
+            now = ahead.reshape(ahead.shape[0] // 8, 8, rows)
+            if b + 1 < videos * tiles:
+                ahead = similarity(b + 1)
+            top = jnp.max(now, axis=0)
+            peaks[b] = top
+            sums[b] = jnp.sum(jnp.exp2((now - top[None]) * SCALE), axis=0)
         for v in range(videos):
-            now = ahead
-            if v + 1 < videos:
-                ahead = similarity(v + 1)
-            peak = jnp.max(now, axis=0, keepdims=True)
-            total = jnp.sum(jnp.exp2((now - peak) * SCALE), axis=0, keepdims=True)
+            tops = peaks[v * tiles : (v + 1) * tiles].reshape(tiles * 8, rows)
+            parts = sums[v * tiles : (v + 1) * tiles].reshape(tiles * 8, rows)
+            peak = jnp.max(tops, axis=0, keepdims=True)
+            total = jnp.sum(parts * jnp.exp2((tops - peak) * SCALE), axis=0, keepdims=True)
             soft[v : v + 1, :] = peak + UNSCALE * jnp.log2(total)
         r = lax.rem(k, rounds)
         first = ((side * 2 + tok) * subs + k // rounds) * (rows // slots)
@@ -354,6 +362,8 @@
             stream, stream, stream, stream, stream,
             pltpu.VMEM((2, videos, 2, tokens, depth), bf16),
             pltpu.VMEM((n, 1, blocks), jnp.int32),
+            pltpu.VMEM((2 * videos, 8, rows), f32),
+            pltpu.VMEM((2 * videos, 8, rows), f32),
             pltpu.VMEM((videos, rows), f32),
             pltpu.VMEM((2, rounds, videos, blocks), f32),
             pltpu.VMEM((3, rounds, videos, blocks), f32),
@@ -362,7 +372,7 @@
             dma((n,)), dma((n,)), dma((5,)), dma((5,)), dma((3,)), dma((3,)),
         ],
         compiler_params=pltpu.CompilerParams(
-            collective_id=0, has_side_effects=True, vmem_limit_bytes=40 * 1024 * 1024
+            collective_id=0, has_side_effects=True, vmem_limit_bytes=64 * 1024 * 1024 - 256 * 1024
         ),
         cost_estimate=pl.CostEstimate(
             flops=2 * depth * logits, bytes_accessed=8 * 1024 * 1024, transcendentals=logits

time: 57.6 us -> 55 us (0.955)
  local copies, waits for them, and re-layouts: 3.5 us -> 1.35 us
    unnamed x9 -> x1, local copies, waits for them, and re-layouts: 3.5 us -> 1.35 us
where the time goes in v3:
time: 55 us; the launch traced here: 54.9 us
  Pallas kernels  53.5 us (97%)
  local copies, waits for them, and re-layouts  1.35 us (2%)
    pallas_call x1, Pallas kernels, per_device(): pl.pallas_call(functools.partial(kernel, n, rounds, slots), out_shape=jax...  53.5 us
    unnamed x1, local copies, waits for them, and re-layouts  1.35 us

profile of v3, /device:TPU:0, one launch (start us, length us, event | category | flops | bytes accessed | tf_op | source)
XLA Modules:
  0.0 54.9 jit_solution(7815251511516227050)
XLA Ops:
  0.0 53.5 %shard_map.46 = f32[12,384]{1,0:T(8,128)} custom-call(bf16[4096,128]{1,0:T(8,128)(2,1)} %bitcast.1, s32[1,128]{1,0:T(1,128)} %counts_ref.1, bf16[12,128,128]{2,1,0:T(8,128)(2,1)} %bank_ref.1, s32[3]{0:T(128)} %owner_ref.1), custom_call_target="tpu_custom_call" | custom-call | flops 4831838208 | bytes 8388608 | tf_op jit(solution)/shard_map/pallas_call | solution.py:350
  53.5 1.3 %copy.6 = f32[12,384]{1,0:T(8,128)} copy(f32[12,384]{1,0:T(8,128)} %shard_map.46) | data formatting | bytes 36864

commit v4 on v3

--- a/solution.py
+++ b/solution.py
@@ -13,7 +13,7 @@
 UNSCALE = math.log(2.0) / sharpness_factor
 
 CHUNK_ROWS = 256
-SKEW = 2
+SKEW = 3
 BANK_LAG = 4
 MESH = pl.DeviceIdType.MESH
 
@@ -168,19 +168,25 @@
         q = query[k].T
         tiles = bank.shape[2]
 
-        def similarity(b):
-            return jnp.dot(
-                bank[slot, b // tiles, b % tiles], q, preferred_element_type=jnp.float32
-            )
+        group = math.gcd(videos, 4)
+
+        def similarity(g):
+            tokens = bank[slot, g * group : (g + 1) * group]
+            tokens = tokens.reshape(group * tiles * bank.shape[3], bank.shape[4])
+            s = jnp.dot(tokens, q, preferred_element_type=jnp.float32)
+            return s.reshape(group * tiles, bank.shape[3] // 8, 8, rows)
 
         ahead = similarity(0)
-        for b in range(videos * tiles):
-            now = ahead.reshape(ahead.shape[0] // 8, 8, rows)
-            if b + 1 < videos * tiles:
-                ahead = similarity(b + 1)
-            top = jnp.max(now, axis=0)
-            peaks[b] = top
-            sums[b] = jnp.sum(jnp.exp2((now - top[None]) * SCALE), axis=0)
+        for g in range(videos // group):
+            now = ahead
+            if (g + 1) * group < videos:
+                ahead = similarity(g + 1)
+            for b in range(group * tiles):
+                top = jnp.max(now[b], axis=0)
+                peaks[g * group * tiles + b] = top
+                sums[g * group * tiles + b] = jnp.sum(
+                    jnp.exp2((now[b] - top[None]) * SCALE), axis=0
+                )
         for v in range(videos):
             tops = peaks[v * tiles : (v + 1) * tiles].reshape(tiles * 8, rows)
             parts = sums[v * tiles : (v + 1) * tiles].reshape(tiles * 8, rows)

time: 55 us -> 54.5 us (level)
  Pallas kernels: 53.5 us -> 52.9 us
    pallas_call x1, Pallas kernels: 53.5 us -> 52.9 us  [per_device(): pl.pallas_call(functools.partial(kernel, n, rounds, slots), out_shape=jax...]
where the time goes in v4:
time: 54.5 us; the launch traced here: 54.3 us
  Pallas kernels  52.9 us (97%)
  local copies, waits for them, and re-layouts  1.35 us (2%)
    pallas_call x1, Pallas kernels, per_device(): pl.pallas_call(functools.partial(kernel, n, rounds, slots), out_shape=jax...  52.9 us
    unnamed x1, local copies, waits for them, and re-layouts  1.35 us

profile of v4, /device:TPU:0, one launch (start us, length us, event | category | flops | bytes accessed | tf_op | source)
XLA Modules:
  0.0 54.3 jit_solution(13107158491044775851)
XLA Ops:
  0.0 52.9 %shard_map.46 = f32[12,384]{1,0:T(8,128)} custom-call(bf16[4096,128]{1,0:T(8,128)(2,1)} %bitcast.1, s32[1,128]{1,0:T(1,128)} %counts_ref.1, bf16[12,128,128]{2,1,0:T(8,128)(2,1)} %bank_ref.1, s32[3]{0:T(128)} %owner_ref.1), custom_call_target="tpu_custom_call" | custom-call | flops 4831838208 | bytes 8388608 | tf_op jit(solution)/shard_map/pallas_call | solution.py:356
  52.9 1.3 %copy.6 = f32[12,384]{1,0:T(8,128)} copy(f32[12,384]{1,0:T(8,128)} %shard_map.46) | data formatting | bytes 36864

commit v5 on v4

--- a/solution.py
+++ b/solution.py
@@ -184,9 +184,8 @@
             for b in range(group * tiles):
                 top = jnp.max(now[b], axis=0)
                 peaks[g * group * tiles + b] = top
-                sums[g * group * tiles + b] = jnp.sum(
-                    jnp.exp2((now[b] - top[None]) * SCALE), axis=0
-                )
+                powers = jnp.exp2(((now[b] - top[None]) * SCALE).astype(jnp.bfloat16))
+                sums[g * group * tiles + b] = jnp.sum(powers.astype(jnp.float32), axis=0)
         for v in range(videos):
             tops = peaks[v * tiles : (v + 1) * tiles].reshape(tiles * 8, rows)
             parts = sums[v * tiles : (v + 1) * tiles].reshape(tiles * 8, rows)

time: 54.5 us -> 66 us (1.21)
  Pallas kernels: 52.9 us -> 64.5 us
    pallas_call x1, Pallas kernels: 52.9 us -> 64.5 us  [per_device(): pl.pallas_call(functools.partial(kernel, n, rounds, slots), out_shape=jax...]
where the time goes in v5:
time: 66 us; the launch traced here: 65.8 us
  Pallas kernels  64.5 us (98%)
  local copies, waits for them, and re-layouts  1.35 us (2%)
    pallas_call x1, Pallas kernels, per_device(): pl.pallas_call(functools.partial(kernel, n, rounds, slots), out_shape=jax...  64.5 us
    unnamed x1, local copies, waits for them, and re-layouts  1.35 us

profile of v5, /device:TPU:0, one launch (start us, length us, event | category | flops | bytes accessed | tf_op | source)
XLA Modules:
  0.0 65.8 jit_solution(6587831708144239236)
XLA Ops:
  0.0 64.5 %shard_map.46 = f32[12,384]{1,0:T(8,128)} custom-call(bf16[4096,128]{1,0:T(8,128)(2,1)} %bitcast.1, s32[1,128]{1,0:T(1,128)} %counts_ref.1, bf16[12,128,128]{2,1,0:T(8,128)(2,1)} %bank_ref.1, s32[3]{0:T(128)} %owner_ref.1), custom_call_target="tpu_custom_call" | custom-call | flops 4831838208 | bytes 8388608 | tf_op jit(solution)/shard_map/pallas_call | solution.py:355
  64.5 1.3 %copy.6 = f32[12,384]{1,0:T(8,128)} copy(f32[12,384]{1,0:T(8,128)} %shard_map.46) | data formatting | bytes 36864

commit v6 on v5

--- a/solution.py
+++ b/solution.py
@@ -21,7 +21,7 @@
 def kernel(
     n, rounds, slots,
     caps_ref, counts_ref, bank_ref, owner_ref, out_ref,
-    mine, in_left, in_right, out_left, out_right, query, bank, counts_all, peaks, sums, soft, acc, acc_in,
+    mine, in_left, in_right, out_left, out_right, query, bank, counts_all, peaks, sums, masks, acc, acc_in,
     own_sem, bank_sem, pair_send, pair_recv, right_send, right_recv, left_send, left_recv,
     count_send, count_recv, bank_send, bank_recv, acc_send, acc_recv,
 ):
@@ -165,7 +165,7 @@
         ).astype(jnp.bfloat16)
 
     def score(k, slot):
-        q = query[k].T
+        q = query[k]
         tiles = bank.shape[2]
 
         group = math.gcd(videos, 4)
@@ -174,38 +174,37 @@
             tokens = bank[slot, g * group : (g + 1) * group]
             tokens = tokens.reshape(group * tiles * bank.shape[3], bank.shape[4])
             s = jnp.dot(tokens, q, preferred_element_type=jnp.float32)
-            return s.reshape(group * tiles, bank.shape[3] // 8, 8, rows)
+            return s.reshape(group, tiles * bank.shape[3] // 8, 8, rows)
 
         ahead = similarity(0)
         for g in range(videos // group):
             now = ahead
             if (g + 1) * group < videos:
                 ahead = similarity(g + 1)
-            for b in range(group * tiles):
+            for b in range(group):
                 top = jnp.max(now[b], axis=0)
-                peaks[g * group * tiles + b] = top
-                powers = jnp.exp2(((now[b] - top[None]) * SCALE).astype(jnp.bfloat16))
-                sums[g * group * tiles + b] = jnp.sum(powers.astype(jnp.float32), axis=0)
-        for v in range(videos):
-            tops = peaks[v * tiles : (v + 1) * tiles].reshape(tiles * 8, rows)
-            parts = sums[v * tiles : (v + 1) * tiles].reshape(tiles * 8, rows)
-            peak = jnp.max(tops, axis=0, keepdims=True)
-            total = jnp.sum(parts * jnp.exp2((tops - peak) * SCALE), axis=0, keepdims=True)
-            soft[v : v + 1, :] = peak + UNSCALE * jnp.log2(total)
+                peaks[g * group + b] = top
+                sums[g * group + b] = jnp.sum(jnp.exp2((now[b] - top[None]) * SCALE), axis=0)
+        tops = peaks[...]
+        peak = jnp.max(tops, axis=1)
+        weighed = sums[...] * jnp.exp2((tops - peak[:, None, :]) * SCALE)
+        values = peak + UNSCALE * jnp.log2(jnp.sum(weighed, axis=1))
         r = lax.rem(k, rounds)
+        keep = masks[k]
+        high = values.astype(jnp.bfloat16)
+        low = (values - high.astype(jnp.float32)).astype(jnp.bfloat16)
+        acc[slot, r] += jnp.dot(high, keep, preferred_element_type=jnp.float32) + jnp.dot(
+            low, keep, preferred_element_type=jnp.float32
+        )
+
+    def mask(k):
         first = ((side * 2 + tok) * subs + k // rounds) * (rows // slots)
         width = acc.shape[3]
         row = lax.broadcasted_iota(jnp.int32, (rows, width), 0)
         column = lax.broadcasted_iota(jnp.int32, (rows, width), 1)
         counts = counts_all[owner_of(k)]
         keep = (column == first + row // slots) & (row % slots < counts)
-        keep = jnp.where(keep, 1.0, 0.0).astype(jnp.bfloat16)
-        values = soft[...]
-        high = values.astype(jnp.bfloat16)
-        low = (values - high.astype(jnp.float32)).astype(jnp.bfloat16)
-        acc[slot, r] += jnp.dot(high, keep, preferred_element_type=jnp.float32) + jnp.dot(
-            low, keep, preferred_element_type=jnp.float32
-        )
+        return jnp.where(keep, 1.0, 0.0).astype(jnp.bfloat16)
 
     near = jnp.minimum(place, line - 1 - place)
     far = jnp.maximum(place, line - 1 - place)
@@ -285,7 +284,8 @@
                 in_left[k].astype(jnp.float32),
                 in_right[k].astype(jnp.float32),
             )
-            query[k] = pick(k, travelled)
+            query[k] = pick(k, travelled).T
+            masks[k] = mask(k)
             score(k, 0)
 
         k_late = k - BANK_LAG
@@ -364,12 +364,13 @@
         out_specs=pl.BlockSpec(memory_space=pltpu.VMEM),
         scratch_shapes=[
             pltpu.VMEM((2, subs, rows, depth), bf16),
-            stream, stream, stream, stream, stream,
+            stream, stream, stream, stream,
+            pltpu.VMEM((chunks, depth, rows), bf16),
             pltpu.VMEM((2, videos, 2, tokens, depth), bf16),
             pltpu.VMEM((n, 1, blocks), jnp.int32),
-            pltpu.VMEM((2 * videos, 8, rows), f32),
-            pltpu.VMEM((2 * videos, 8, rows), f32),
-            pltpu.VMEM((videos, rows), f32),
+            pltpu.VMEM((videos, 8, rows), f32),
+            pltpu.VMEM((videos, 8, rows), f32),
+            pltpu.VMEM((chunks, rows, blocks), bf16),
             pltpu.VMEM((2, rounds, videos, blocks), f32),
             pltpu.VMEM((3, rounds, videos, blocks), f32),
             dma((subs,)), dma, dma((subs,)), dma((subs,)),

time: 66 us -> 56 us (0.85)
  Pallas kernels: 64.5 us -> 54.5 us
    pallas_call x1, Pallas kernels: 64.5 us -> 54.5 us  [per_device(): pl.pallas_call(functools.partial(kernel, n, rounds, slots), out_shape=jax...]
where the time goes in v6:
time: 56 us; the launch traced here: 55.9 us
  Pallas kernels  54.5 us (97%)
  local copies, waits for them, and re-layouts  1.35 us (2%)
    pallas_call x1, Pallas kernels, per_device(): pl.pallas_call(functools.partial(kernel, n, rounds, slots), out_shape=jax...  54.5 us
    unnamed x1, local copies, waits for them, and re-layouts  1.35 us

profile of v6, /device:TPU:0, one launch (start us, length us, event | category | flops | bytes accessed | tf_op | source)
XLA Modules:
  0.0 55.9 jit_solution(5920269492703274860)
XLA Ops:
  0.0 54.5 %shard_map.46 = f32[12,384]{1,0:T(8,128)} custom-call(bf16[4096,128]{1,0:T(8,128)(2,1)} %bitcast.1, s32[1,128]{1,0:T(1,128)} %counts_ref.1, bf16[12,128,128]{2,1,0:T(8,128)(2,1)} %bank_ref.1, s32[3]{0:T(128)} %owner_ref.1), custom_call_target="tpu_custom_call" | custom-call | flops 4831838208 | bytes 8388608 | tf_op jit(solution)/shard_map/pallas_call | solution.py:355
  54.5 1.3 %copy.6 = f32[12,384]{1,0:T(8,128)} copy(f32[12,384]{1,0:T(8,128)} %shard_map.46) | data formatting | bytes 36864

commit v7 on v6

--- a/solution.py
+++ b/solution.py
@@ -13,6 +13,7 @@
 UNSCALE = math.log(2.0) / sharpness_factor
 
 CHUNK_ROWS = 256
+LANES = 128
 SKEW = 3
 BANK_LAG = 4
 MESH = pl.DeviceIdType.MESH
@@ -174,17 +175,21 @@
             tokens = bank[slot, g * group : (g + 1) * group]
             tokens = tokens.reshape(group * tiles * bank.shape[3], bank.shape[4])
             s = jnp.dot(tokens, q, preferred_element_type=jnp.float32)
-            return s.reshape(group, tiles * bank.shape[3] // 8, 8, rows)
+            return s.reshape(group * tiles, bank.shape[3] // 8, 8, rows)
 
         ahead = similarity(0)
         for g in range(videos // group):
             now = ahead
             if (g + 1) * group < videos:
                 ahead = similarity(g + 1)
-            for b in range(group):
-                top = jnp.max(now[b], axis=0)
-                peaks[g * group + b] = top
-                sums[g * group + b] = jnp.sum(jnp.exp2((now[b] - top[None]) * SCALE), axis=0)
+            for b in range(group * tiles):
+                for lane in range(0, rows, LANES):
+                    block = now[b, :, :, lane : lane + LANES]
+                    top = jnp.max(block, axis=0)
+                    powers = jnp.exp2((block - top[None]) * SCALE)
+                    video, tile = divmod(g * group * tiles + b, tiles)
+                    peaks[video, tile * 8 : tile * 8 + 8, lane : lane + LANES] = top
+                    sums[video, tile * 8 : tile * 8 + 8, lane : lane + LANES] = jnp.sum(powers, axis=0)
         tops = peaks[...]
         peak = jnp.max(tops, axis=1)
         weighed = sums[...] * jnp.exp2((tops - peak[:, None, :]) * SCALE)
@@ -368,8 +373,8 @@
             pltpu.VMEM((chunks, depth, rows), bf16),
             pltpu.VMEM((2, videos, 2, tokens, depth), bf16),
             pltpu.VMEM((n, 1, blocks), jnp.int32),
-            pltpu.VMEM((videos, 8, rows), f32),
-            pltpu.VMEM((videos, 8, rows), f32),
+            pltpu.VMEM((videos, 16, rows), f32),
+            pltpu.VMEM((videos, 16, rows), f32),
             pltpu.VMEM((chunks, rows, blocks), bf16),
             pltpu.VMEM((2, rounds, videos, blocks), f32),
             pltpu.VMEM((3, rounds, videos, blocks), f32),

time: 56 us -> 53.6 us (0.957)
  Pallas kernels: 54.5 us -> 52.1 us
    pallas_call x1, Pallas kernels: 54.5 us -> 52.1 us  [per_device(): pl.pallas_call(functools.partial(kernel, n, rounds, slots), out_shape=jax...]
where the time goes in v7:
time: 53.6 us; the launch traced here: 53.4 us
  Pallas kernels  52.1 us (97%)
  local copies, waits for them, and re-layouts  1.35 us (3%)
    pallas_call x1, Pallas kernels, per_device(): pl.pallas_call(functools.partial(kernel, n, rounds, slots), out_shape=jax...  52.1 us
    unnamed x1, local copies, waits for them, and re-layouts  1.35 us

profile of v7, /device:TPU:0, one launch (start us, length us, event | category | flops | bytes accessed | tf_op | source)
XLA Modules:
  0.0 53.4 jit_solution(12919185320803836348)
XLA Ops:
  0.0 52.1 %shard_map.46 = f32[12,384]{1,0:T(8,128)} custom-call(bf16[4096,128]{1,0:T(8,128)(2,1)} %bitcast.1, s32[1,128]{1,0:T(1,128)} %counts_ref.1, bf16[12,128,128]{2,1,0:T(8,128)(2,1)} %bank_ref.1, s32[3]{0:T(128)} %owner_ref.1), custom_call_target="tpu_custom_call" | custom-call | flops 4831838208 | bytes 8388608 | tf_op jit(solution)/shard_map/pallas_call | solution.py:360
  52.1 1.3 %copy.6 = f32[12,384]{1,0:T(8,128)} copy(f32[12,384]{1,0:T(8,128)} %shard_map.46) | data formatting | bytes 36864

commit v8 on v7

--- a/solution.py
+++ b/solution.py
@@ -14,7 +14,8 @@
 
 CHUNK_ROWS = 256
 LANES = 128
-SKEW = 3
+SKEW = 2
+PIECES = 2
 BANK_LAG = 4
 MESH = pl.DeviceIdType.MESH
 
@@ -97,14 +98,20 @@
             bank_send.at[3 + i], bank_recv.at[3 + i], twin_id,
         )
 
-    def right_copy(k):
-        return remote(
-            out_right.at[k], in_left.at[k], right_send.at[k], right_recv.at[k], right_id
-        )
-
-    def left_copy(k):
-        return remote(
-            out_left.at[k], in_right.at[k], left_send.at[k], left_recv.at[k], left_id
+    def piece(h):
+        size = rows // PIECES
+        return pl.ds(h * size, size)
+
+    def right_copy(k, h):
+        return remote(
+            out_right.at[k, piece(h)], in_left.at[k, piece(h)],
+            right_send.at[k, h], right_recv.at[k, h], right_id,
+        )
+
+    def left_copy(k, h):
+        return remote(
+            out_left.at[k, piece(h)], in_right.at[k, piece(h)],
+            left_send.at[k, h], left_recv.at[k, h], left_id,
         )
 
     def count_copy(to):
@@ -148,21 +155,17 @@
     def owner_of(k):
         return owner_ref[lax.rem(k, rounds)]
 
-    def candidate(k):
+    def candidate(k, span):
         sub = k // rounds
-        owner_side = jnp.full((rows, mine.shape[3]), lax.rem(owner_of(k), 2), jnp.int32)
+        first = mine[0, sub, span].astype(jnp.float32)
+        second = mine[1, sub, span].astype(jnp.float32)
+        owner_side = jnp.full(first.shape, lax.rem(owner_of(k), 2), jnp.int32)
+        return jnp.where(owner_side == 0, first, second)
+
+    def pick(k, incoming, span):
+        owner_place = jnp.full(incoming.shape, owner_of(k) // 2, jnp.int32)
         return jnp.where(
-            owner_side == 0,
-            mine[0, sub].astype(jnp.float32),
-            mine[1, sub].astype(jnp.float32),
-        )
-
-    def owner_place(k):
-        return jnp.full((rows, mine.shape[3]), owner_of(k) // 2, jnp.int32)
-
-    def pick(k, incoming):
-        return jnp.where(
-            owner_place(k) == place, candidate(k), incoming.astype(jnp.float32)
+            owner_place == place, candidate(k, span), incoming.astype(jnp.float32)
         ).astype(jnp.bfloat16)
 
     def score(k, slot):
@@ -236,27 +239,43 @@
 
         @pl.when((k_right >= 0) & (k_right < chunks))
         def _():
-            @pl.when(place > 0)
-            def _():
-                right_copy(k_right).wait_recv()
-
-            @pl.when(place < line - 1)
-            def _():
-                out_right[k_right] = pick(k_right, in_left[k_right])
-                right_copy(k_right).start()
+            for h in range(PIECES):
+                @pl.when(place > 0)
+                def _():
+                    right_copy(k_right, h).wait_recv()
+
+                @pl.when(place < line - 1)
+                def _():
+                    out_right[k_right, piece(h)] = pick(
+                        k_right, in_left[k_right, piece(h)], piece(h)
+                    )
+
+                    @pl.when(k_right > 0)
+                    def _():
+                        right_copy(k_right - 1, h).wait_send()
+
+                    right_copy(k_right, h).start()
 
         k_left = step - SKEW * (line - 1 - place)
 
         @pl.when((k_left >= 0) & (k_left < chunks))
         def _():
-            @pl.when(place < line - 1)
-            def _():
-                left_copy(k_left).wait_recv()
-
-            @pl.when(place > 0)
-            def _():
-                out_left[k_left] = pick(k_left, in_right[k_left])
-                left_copy(k_left).start()
+            for h in range(PIECES):
+                @pl.when(place < line - 1)
+                def _():
+                    left_copy(k_left, h).wait_recv()
+
+                @pl.when(place > 0)
+                def _():
+                    out_left[k_left, piece(h)] = pick(
+                        k_left, in_right[k_left, piece(h)], piece(h)
+                    )
+
+                    @pl.when(k_left > 0)
+                    def _():
+                        left_copy(k_left - 1, h).wait_send()
+
+                    left_copy(k_left, h).start()
 
         k = step - SKEW * far
 
@@ -285,11 +304,11 @@
         @pl.when((k >= 0) & (k < chunks))
         def _():
             travelled = jnp.where(
-                owner_place(k) < place,
+                jnp.full(in_left.shape[1:], owner_of(k) // 2, jnp.int32) < place,
                 in_left[k].astype(jnp.float32),
                 in_right[k].astype(jnp.float32),
             )
-            query[k] = pick(k, travelled).T
+            query[k] = pick(k, travelled, pl.ds(0, rows)).T
             masks[k] = mask(k)
             score(k, 0)
 
@@ -323,18 +342,15 @@
         bank_pair(i).wait_send()
         bank_relay(i).wait_send()
 
-    def drain(k, _):
+    for h in range(PIECES):
         @pl.when(place < line - 1)
         def _():
-            right_copy(k).wait_send()
+            right_copy(chunks - 1, h).wait_send()
 
         @pl.when(place > 0)
         def _():
-            left_copy(k).wait_send()
-
-        return 0
-
-    lax.fori_loop(0, chunks, drain, 0)
+            left_copy(chunks - 1, h).wait_send()
+
     for send in sends:
         send.wait()
     width = acc.shape[3]
@@ -379,7 +395,8 @@
             pltpu.VMEM((2, rounds, videos, blocks), f32),
             pltpu.VMEM((3, rounds, videos, blocks), f32),
             dma((subs,)), dma, dma((subs,)), dma((subs,)),
-            dma((chunks,)), dma((chunks,)), dma((chunks,)), dma((chunks,)),
+            dma((chunks, PIECES)), dma((chunks, PIECES)),
+            dma((chunks, PIECES)), dma((chunks, PIECES)),
             dma((n,)), dma((n,)), dma((5,)), dma((5,)), dma((3,)), dma((3,)),
         ],
         compiler_params=pltpu.CompilerParams(

time: 53.6 us -> 55.6 us (1.037)
  Pallas kernels: 52.1 us -> 54.1 us
    pallas_call x1, Pallas kernels: 52.1 us -> 54.1 us  [per_device(): pl.pallas_call(functools.partial(kernel, n, rounds, slots), out_shape=jax...]
where the time goes in v8:
time: 55.6 us; the launch traced here: 55.4 us
  Pallas kernels  54.1 us (97%)
  local copies, waits for them, and re-layouts  1.35 us (2%)
    pallas_call x1, Pallas kernels, per_device(): pl.pallas_call(functools.partial(kernel, n, rounds, slots), out_shape=jax...  54.1 us
    unnamed x1, local copies, waits for them, and re-layouts  1.35 us

profile of v8, /device:TPU:0, one launch (start us, length us, event | category | flops | bytes accessed | tf_op | source)
XLA Modules:
  0.0 55.4 jit_solution(9112244213304080489)
XLA Ops:
  0.0 54.1 %shard_map.46 = f32[12,384]{1,0:T(8,128)} custom-call(bf16[4096,128]{1,0:T(8,128)(2,1)} %bitcast.1, s32[1,128]{1,0:T(1,128)} %counts_ref.1, bf16[12,128,128]{2,1,0:T(8,128)(2,1)} %bank_ref.1, s32[3]{0:T(128)} %owner_ref.1), custom_call_target="tpu_custom_call" | custom-call | flops 4831838208 | bytes 8388608 | tf_op jit(solution)/shard_map/pallas_call | solution.py:376
  54.1 1.3 %copy.6 = f32[12,384]{1,0:T(8,128)} copy(f32[12,384]{1,0:T(8,128)} %shard_map.46) | data formatting | bytes 36864

commit v9 on v7

--- a/solution.py
+++ b/solution.py
@@ -174,6 +174,7 @@
         def similarity(g):
             tokens = bank[slot, g * group : (g + 1) * group]
             tokens = tokens.reshape(group * tiles * bank.shape[3], bank.shape[4])
+            tokens = jnp.concatenate([tokens, tokens], axis=1)
             s = jnp.dot(tokens, q, preferred_element_type=jnp.float32)
             return s.reshape(group * tiles, bank.shape[3] // 8, 8, rows)
 
@@ -186,14 +187,14 @@
                 for lane in range(0, rows, LANES):
                     block = now[b, :, :, lane : lane + LANES]
                     top = jnp.max(block, axis=0)
-                    powers = jnp.exp2((block - top[None]) * SCALE)
+                    powers = jnp.exp2(block - top[None])
                     video, tile = divmod(g * group * tiles + b, tiles)
                     peaks[video, tile * 8 : tile * 8 + 8, lane : lane + LANES] = top
                     sums[video, tile * 8 : tile * 8 + 8, lane : lane + LANES] = jnp.sum(powers, axis=0)
         tops = peaks[...]
         peak = jnp.max(tops, axis=1)
-        weighed = sums[...] * jnp.exp2((tops - peak[:, None, :]) * SCALE)
-        values = peak + UNSCALE * jnp.log2(jnp.sum(weighed, axis=1))
+        weighed = sums[...] * jnp.exp2(tops - peak[:, None, :])
+        values = UNSCALE * (peak + jnp.log2(jnp.sum(weighed, axis=1)))
         r = lax.rem(k, rounds)
         keep = masks[k]
         high = values.astype(jnp.bfloat16)
@@ -289,7 +290,10 @@
                 in_left[k].astype(jnp.float32),
                 in_right[k].astype(jnp.float32),
             )
-            query[k] = pick(k, travelled).T
+            scaled = pick(k, travelled).astype(jnp.float32) * SCALE
+            upper = scaled.astype(jnp.bfloat16)
+            lower = (scaled - upper.astype(jnp.float32)).astype(jnp.bfloat16)
+            query[k] = jnp.concatenate([upper.T, lower.T], axis=0)
             masks[k] = mask(k)
             score(k, 0)
 
@@ -370,7 +374,7 @@
         scratch_shapes=[
             pltpu.VMEM((2, subs, rows, depth), bf16),
             stream, stream, stream, stream,
-            pltpu.VMEM((chunks, depth, rows), bf16),
+            pltpu.VMEM((chunks, 2 * depth, rows), bf16),
             pltpu.VMEM((2, videos, 2, tokens, depth), bf16),
             pltpu.VMEM((n, 1, blocks), jnp.int32),
             pltpu.VMEM((videos, 16, rows), f32),

time: 53.6 us -> 52.7 us (0.983)
  Pallas kernels: 52.1 us -> 51.2 us
    pallas_call x1, Pallas kernels: 52.1 us -> 51.2 us  [per_device(): pl.pallas_call(functools.partial(kernel, n, rounds, slots), out_shape=jax...]
where the time goes in v9:
time: 52.7 us; the launch traced here: 52.5 us
  Pallas kernels  51.2 us (97%)
  local copies, waits for them, and re-layouts  1.35 us (3%)
    pallas_call x1, Pallas kernels, per_device(): pl.pallas_call(functools.partial(kernel, n, rounds, slots), out_shape=jax...  51.2 us
    unnamed x1, local copies, waits for them, and re-layouts  1.35 us

profile of v9, /device:TPU:0, one launch (start us, length us, event | category | flops | bytes accessed | tf_op | source)
XLA Modules:
  0.0 52.5 jit_solution(3284412041643483644)
XLA Ops:
  0.0 51.2 %shard_map.46 = f32[12,384]{1,0:T(8,128)} custom-call(bf16[4096,128]{1,0:T(8,128)(2,1)} %bitcast.1, s32[1,128]{1,0:T(1,128)} %counts_ref.1, bf16[12,128,128]{2,1,0:T(8,128)(2,1)} %bank_ref.1, s32[3]{0:T(128)} %owner_ref.1), custom_call_target="tpu_custom_call" | custom-call | flops 4831838208 | bytes 8388608 | tf_op jit(solution)/shard_map/pallas_call | solution.py:364
  51.2 1.3 %copy.6 = f32[12,384]{1,0:T(8,128)} copy(f32[12,384]{1,0:T(8,128)} %shard_map.46) | data formatting | bytes 36864

commit v10 on v9

--- a/solution.py
+++ b/solution.py
@@ -14,7 +14,7 @@
 
 CHUNK_ROWS = 256
 LANES = 128
-SKEW = 3
+SKEW = 4
 BANK_LAG = 4
 MESH = pl.DeviceIdType.MESH
 

time: 52.7 us -> 53.8 us (1.021)
  Pallas kernels: 51.2 us -> 52.2 us
    pallas_call x1, Pallas kernels: 51.2 us -> 52.2 us  [per_device(): pl.pallas_call(functools.partial(kernel, n, rounds, slots), out_shape=jax...]
where the time goes in v10:
time: 53.8 us; the launch traced here: 53.6 us
  Pallas kernels  52.2 us (97%)
  local copies, waits for them, and re-layouts  1.35 us (3%)
    pallas_call x1, Pallas kernels, per_device(): pl.pallas_call(functools.partial(kernel, n, rounds, slots), out_shape=jax...  52.2 us
    unnamed x1, local copies, waits for them, and re-layouts  1.35 us

profile of v10, /device:TPU:0, one launch (start us, length us, event | category | flops | bytes accessed | tf_op | source)
XLA Modules:
  0.0 53.6 jit_solution(6876097691152846261)
XLA Ops:
  0.0 52.2 %shard_map.46 = f32[12,384]{1,0:T(8,128)} custom-call(bf16[4096,128]{1,0:T(8,128)(2,1)} %bitcast.1, s32[1,128]{1,0:T(1,128)} %counts_ref.1, bf16[12,128,128]{2,1,0:T(8,128)(2,1)} %bank_ref.1, s32[3]{0:T(128)} %owner_ref.1), custom_call_target="tpu_custom_call" | custom-call | flops 4831838208 | bytes 8388608 | tf_op jit(solution)/shard_map/pallas_call | solution.py:364
  52.2 1.3 %copy.6 = f32[12,384]{1,0:T(8,128)} copy(f32[12,384]{1,0:T(8,128)} %shard_map.46) | data formatting | bytes 36864
